TPU v7x, 32 devices: a whole 2x2x4 slice. The times are simulated.
32 devices in a mesh: parts: 2 (over y), row: 16 (over z, x, core).
Axes of the slice: x: 2, y: 2, z: 4, core: 2. Of those that a mesh axis runs over, the one named last changes fastest.
Arguments:
- traces: bfloat16 [256, 2, 12000], P(('parts', 'row')), parts along dimension 0, may hold values from -160 to 160
- valid_mask: int32 [256, 2], P(('parts', 'row')), parts along dimension 0, may hold values 0 or 1
- pair_table: int32 [32, 10], P(('parts', 'row')), parts along dimension 0, may hold values from 0 to 15, as said below
- stack_in: float32 [32, 10, 8, 8, 401], P(('parts', 'row')), parts along dimension 0, may hold values from -6 to 6
Outputs:
- stacks: float32 [32, 10, 8, 8, 401], P(('parts', 'row')), parts along dimension 0
There are 2 independent parts, one for each index of `parts`. A program takes and returns all parts, laid end to end along the dimension named above; each array names one. Nothing has to cross between parts.
Inputs may be any that keep to these rules, and one draw needn't show every extreme that they name: `pair_table`: row i lists the panels (i + k) mod 16 for k = -1 to 8, each once, in an order that varies from row to row.
All inputs are finite; a program needn't handle non-finite values. No bound on the sum of `valid_mask` on one device may be relied on, other than what follows from the above.
Results may differ from a plain program's by a relative error of at most 0.0032.
Values may be sent and summed in bfloat16 or wider, within the bound.
A program may use at most 128 MiB of HBM per device.

v0:
```python
import math

import jax
import jax.numpy as jnp
from jax import lax
from jax.sharding import PartitionSpec as P

SAMPLES = 12000
FLO = 6
BINS = 595
HALF = 40
LAGS = 401


epsilon = 1e-06


def spectra_of(rows, samples, first_bin, bins):
    length = samples // 8
    freq = first_bin + jnp.arange(bins, dtype=jnp.int32)

    def absorb(totals, block_index):
        first_row = block_index * length
        segment = lax.dynamic_slice_in_dim(rows, first_row, length, 1)
        times = first_row + jnp.arange(length, dtype=jnp.int32)
        angle = (times[:, None] * freq[None, :] % samples).astype(jnp.float32) * (
            2.0 * math.pi / samples
        )
        table = jnp.concatenate([jnp.cos(angle), -jnp.sin(angle)], axis=1).astype(jnp.bfloat16)
        return (totals + jnp.dot(segment, table, preferred_element_type=jnp.float32), None)

    start_total = jnp.zeros((rows.shape[0], 2 * bins), jnp.float32)
    totals, unused = lax.scan(absorb, start_total, jnp.arange(8, dtype=jnp.int32))
    return totals


def whiten_rows(traces, valid_mask, first_bin, bins, half_width):
    chans, minutes, samples = traces.shape
    spectrum = spectra_of(traces.reshape(chans * minutes, samples), samples, first_bin, bins)
    real_part = spectrum[:, :bins]
    imag_part = spectrum[:, bins:]
    power = real_part * real_part + imag_part * imag_part
    positions = jnp.arange(bins, dtype=jnp.int32)
    near = (jnp.abs(positions[:, None] - positions[None, :]) <= half_width).astype(jnp.float32)
    window = near / jnp.sum(near, axis=0, keepdims=True)
    smooth = jnp.dot(power, window, precision=lax.Precision.HIGHEST)
    divisor = jnp.sqrt(smooth + epsilon)
    flags = valid_mask.reshape(-1, 1).astype(jnp.float32)
    whitened = spectrum * flags / jnp.concatenate([divisor, divisor], axis=1)
    return whitened.astype(jnp.bfloat16).reshape(chans, minutes, 2 * bins)


def lag_matrix(first_bin, bins, lags, samples):
    freq = first_bin + jnp.arange(bins, dtype=jnp.int32)
    shifts = jnp.arange(lags, dtype=jnp.int32) - (lags - 1) // 2
    angle = (freq[:, None] * shifts[None, :] % samples).astype(jnp.float32) * (
        2.0 * math.pi / samples
    )
    return jnp.concatenate([jnp.cos(angle), -jnp.sin(angle)], axis=0).astype(jnp.bfloat16)


def tile_corr(own_white, own_flags, partner_white, partner_flags, lag_table):
    bins = lag_table.shape[0] // 2
    own = own_white.astype(jnp.float32)
    partner = partner_white.astype(jnp.float32)
    shape = (partner.shape[0], own.shape[0], partner.shape[1], bins)
    real_sum = jnp.zeros(shape, jnp.float32)
    imag_sum = jnp.zeros(shape, jnp.float32)
    joint_sum = jnp.zeros(shape[:3], jnp.float32)
    for minute in range(own.shape[1]):
        own_real = own[:, minute, :bins][None, :, None, :]
        own_imag = own[:, minute, bins:][None, :, None, :]
        part_real = partner[:, :, minute, :bins][:, None, :, :]
        part_imag = partner[:, :, minute, bins:][:, None, :, :]
        real_sum = real_sum + (own_real * part_real + own_imag * part_imag)
        imag_sum = imag_sum + (own_imag * part_real - own_real * part_imag)
        own_valid = own_flags[:, minute].astype(jnp.float32)[None, :, None]
        part_valid = partner_flags[:, :, minute].astype(jnp.float32)[:, None, :]
        joint_sum = joint_sum + own_valid * part_valid
    inverse = 1.0 / jnp.maximum(joint_sum, 1.0)
    cross = (jnp.concatenate([real_sum, imag_sum], axis=-1) * inverse[..., None]).astype(
        jnp.bfloat16
    )
    corr = jnp.dot(cross.reshape(-1, 2 * bins), lag_table, preferred_element_type=jnp.float32) * (
        1.0 / math.sqrt(bins)
    )
    return corr.reshape(shape[0], shape[1], shape[2], lag_table.shape[1])


def shards(traces, valid_mask, pair_table, stack_in):
    panel_count = lax.axis_size("row")
    chans = traces.shape[0]
    minutes = traces.shape[1]
    whitened = whiten_rows(traces, valid_mask, FLO, BINS, HALF)
    own_flags = valid_mask.astype(jnp.bfloat16)
    lag_table = lag_matrix(FLO, BINS, LAGS, SAMPLES)
    table_row = pair_table[0]
    base_stack = stack_in[0]
    whole_white, whole_flags = (
        lax.all_gather(whitened, "row", axis=0, tiled=True),
        lax.all_gather(own_flags, "row", axis=0, tiled=True),
    )
    panels = whole_white.reshape(panel_count, chans, minutes, whitened.shape[2])
    panel_flags = whole_flags.reshape(panel_count, chans, minutes)
    partner = jnp.take(panels, table_row, axis=0)
    partner_flags = jnp.take(panel_flags, table_row, axis=0)
    result = base_stack + tile_corr(whitened, own_flags, partner, partner_flags, lag_table)
    return result[None]


def solution(mesh):
    in_specs = (
        P(("parts", "row"), None, None),
        P(("parts", "row"), None),
        P(("parts", "row"), None),
        P(("parts", "row"), None, None, None, None),
    )
    out_specs = P(("parts", "row"), None, None, None, None)
    return jax.shard_map(shards, mesh=mesh, in_specs=in_specs, out_specs=out_specs, check_vma=False)
```

profile of v0, /device:TPU:0, one launch (start us, length us, event | category | flops | bytes accessed | tf_op | source)
XLA Modules:
  0.0 214.5 jit_solution(12585721607296174629)
XLA Ops:
  0.0 0.7 compare_and_fusion
  0.7 0.7 fusion.46
  1.3 0.8 fusion.52
  2.3 0.1 convert_reduce_fusion
  2.4 23.0 %all-gather = bf16[16,8,2]{1,2,0:T(2,128)(2,1)S(1)} all-gather(bf16[1,8,2]{1,2,0:T(2,128)(2,1)S(1)} %bitcast.50), channel_id=1, replica_groups=mesh['parts'=2,'row'=16] {'row'}, dimensions={0}, use_global_device_ids=true | all-gather | bytes 544 | tf_op jit(solution)/shard_map/all_gather | solution.py:101
  25.4 0.6 gather_fusion.1
  25.9 0.1 copy.34
  26.1 0.1 copy.35
  26.2 0.1 maximum_divide_fusion.1
  26.3 0.1 div.25
  26.4 1.3 reshape.162
  27.7 151.3 %while.13 = (s32[]{:T(128)}, f32[16,1190]{1,0:T(8,128)S(1)}, s32[8]{0:T(128)S(1)}, bf16[16,12000]{1,0:T(8,128)(2,1)S(1)}, s32[]{:T(128)}, /*index=5*/s32[1]{0:T(128)}, s32[]{:T(128)}, s32[]{:T(128)}) while((s32[]{:T(128)}, f32[16,1190]{1,0:T(8,128)S(1)}, s32[8]{0:T(128)S(1)}, bf16[16,12000]{1,0:T(8,128)(2,1)S(1)}, s32[]{:T(128)}, ...), condition=%wide.region_1.2_spmd.clone, body=%wide.region_0.1_spmd.clone.sunk | while | flops 75010184 | bytes 7644401 | solution.py:33
  27.7 0.7 dynamic_slice.20
  29.0 16.6 %cosine_convert_fusion.3 = (bf16[1500,595]{1,0:T(8,128)(2,1)S(1)}, bf16[1500,595]{1,0:T(8,128)(2,1)S(1)}) fusion(s32[595]{0:T(1024)S(1)} %iota_add_fusion.6, s32[1500]{0:T(1024)S(1)} %iota_add_fusion.7), kind=kLoop, calls=%fused_computation.11.clone.1 | loop fusion | flops 10710000 | bytes 3578380 | tf_op jit(solution)/shard_map/convert
  45.6 1.0 fusion.58
  46.6 0.6 dynamic_slice.20
  47.9 16.6 %cosine_convert_fusion.3 = (bf16[1500,595]{1,0:T(8,128)(2,1)S(1)}, bf16[1500,595]{1,0:T(8,128)(2,1)S(1)}) fusion(s32[595]{0:T(1024)S(1)} %iota_add_fusion.6, s32[1500]{0:T(1024)S(1)} %iota_add_fusion.7), kind=kLoop, calls=%fused_computation.11.clone.1 | loop fusion | flops 10710000 | bytes 3578380 | tf_op jit(solution)/shard_map/convert
  64.5 1.0 fusion.58
  65.5 0.6 dynamic_slice.20
  66.8 16.6 %cosine_convert_fusion.3 = (bf16[1500,595]{1,0:T(8,128)(2,1)S(1)}, bf16[1500,595]{1,0:T(8,128)(2,1)S(1)}) fusion(s32[595]{0:T(1024)S(1)} %iota_add_fusion.6, s32[1500]{0:T(1024)S(1)} %iota_add_fusion.7), kind=kLoop, calls=%fused_computation.11.clone.1 | loop fusion | flops 10710000 | bytes 3578380 | tf_op jit(solution)/shard_map/convert
  83.4 1.0 fusion.58
  84.4 0.6 dynamic_slice.20
  85.7 16.6 %cosine_convert_fusion.3 = (bf16[1500,595]{1,0:T(8,128)(2,1)S(1)}, bf16[1500,595]{1,0:T(8,128)(2,1)S(1)}) fusion(s32[595]{0:T(1024)S(1)} %iota_add_fusion.6, s32[1500]{0:T(1024)S(1)} %iota_add_fusion.7), kind=kLoop, calls=%fused_computation.11.clone.1 | loop fusion | flops 10710000 | bytes 3578380 | tf_op jit(solution)/shard_map/convert
  102.3 1.0 fusion.58
  103.3 0.6 dynamic_slice.20
  104.6 16.6 %cosine_convert_fusion.3 = (bf16[1500,595]{1,0:T(8,128)(2,1)S(1)}, bf16[1500,595]{1,0:T(8,128)(2,1)S(1)}) fusion(s32[595]{0:T(1024)S(1)} %iota_add_fusion.6, s32[1500]{0:T(1024)S(1)} %iota_add_fusion.7), kind=kLoop, calls=%fused_computation.11.clone.1 | loop fusion | flops 10710000 | bytes 3578380 | tf_op jit(solution)/shard_map/convert
  121.2 1.0 fusion.58
  122.2 0.6 dynamic_slice.20
  123.5 16.6 %cosine_convert_fusion.3 = (bf16[1500,595]{1,0:T(8,128)(2,1)S(1)}, bf16[1500,595]{1,0:T(8,128)(2,1)S(1)}) fusion(s32[595]{0:T(1024)S(1)} %iota_add_fusion.6, s32[1500]{0:T(1024)S(1)} %iota_add_fusion.7), kind=kLoop, calls=%fused_computation.11.clone.1 | loop fusion | flops 10710000 | bytes 3578380 | tf_op jit(solution)/shard_map/convert
  140.1 1.0 fusion.58
  141.1 0.6 dynamic_slice.20
  142.4 16.6 %cosine_convert_fusion.3 = (bf16[1500,595]{1,0:T(8,128)(2,1)S(1)}, bf16[1500,595]{1,0:T(8,128)(2,1)S(1)}) fusion(s32[595]{0:T(1024)S(1)} %iota_add_fusion.6, s32[1500]{0:T(1024)S(1)} %iota_add_fusion.7), kind=kLoop, calls=%fused_computation.11.clone.1 | loop fusion | flops 10710000 | bytes 3578380 | tf_op jit(solution)/shard_map/convert
  159.0 1.0 fusion.58
  160.0 0.6 dynamic_slice.20
  161.3 16.6 %cosine_convert_fusion.3 = (bf16[1500,595]{1,0:T(8,128)(2,1)S(1)}, bf16[1500,595]{1,0:T(8,128)(2,1)S(1)}) fusion(s32[595]{0:T(1024)S(1)} %iota_add_fusion.6, s32[1500]{0:T(1024)S(1)} %iota_add_fusion.7), kind=kLoop, calls=%fused_computation.11.clone.1 | loop fusion | flops 10710000 | bytes 3578380 | tf_op jit(solution)/shard_map/convert
  177.9 1.0 fusion.58
  179.0 0.8 fusion.34
  179.8 0.1 fusion.38
  179.9 0.1 fusion.51
  180.1 19.4 %all_gather.6 = bf16[128,2,1190]{2,1,0:T(2,128)(2,1)S(1)} all-gather(bf16[8,2,1190]{2,1,0:T(2,128)(2,1)S(1)} %reshape.163), channel_id=1, replica_groups=mesh['parts'=2,'row'=16] {'row'}, dimensions={0}, use_global_device_ids=true | all-gather | bytes 647360 | tf_op jit(solution)/shard_map/all_gather | solution.py:100
  199.4 1.4 gather_fusion
  200.9 0.4 fusion.37
  201.3 1.2 fusion.50
  202.6 5.6 %cosine_convert_fusion.1 = (bf16[595,401]{1,0:T(8,128)(2,1)S(1)}, bf16[595,401]{1,0:T(8,128)(2,1)S(1)}) fusion(s32[401]{0:T(512)S(1)} %iota_add_fusion.3, s32[595]{0:T(1024)S(1)} %iota_add_fusion.2), kind=kLoop, calls=%fused_computation.37 | loop fusion | flops 2863140 | bytes 958364 | tf_op jit(solution)/shard_map/convert.6
  208.1 0.8 add_add_fusion
  208.9 2.4 %fusion.22 = f32[640,401]{0,1:T(8,128)} fusion(f32[640,595]{1,0:T(8,128)S(1)} %bitcast.49, f32[640,595]{1,0:T(8,128)S(1)} %bitcast.48, f32[640]{0:T(1024)S(1)} %div.25, bf16[595,401]{1,0:T(8,128)(2,1)S(1)} %get-tuple-element.110, bf16[595,401]{1,0:T(8,128)(2,1)S(1)} %get-tuple-element.109), kind=kOutput, calls=%fused_computation.33 | convolution fusion | flops 615253376 | bytes 5029900 | tf_op jit(solution)/shard_map/dot_general | solution.py:84
  211.3 1.7 copy.37
  213.1 1.4 add.141
  (34 shorter events, 0.5 us)
Async XLA Ops:
  211.3 1.7 copy-start
where the time goes:
time: 215 us; the launch traced here: 214 us
  other arithmetic  143 us (67%)
  blocking collectives  42.3 us (20%)
  local copies, waits for them, and re-layouts  12.1 us (6%)
  matrix products  11.3 us (5%)
  loops' own time  5.26 us (2%)
    another operation x9, other arithmetic  138 us
    all_gather x1, blocking collectives, shards(): lax.all_gather(own_flags, 'row', axis=0, tiled=True)  23 us
    all_gather x1, blocking collectives, shards(): lax.all_gather(whitened, 'row', axis=0, tiled=True)  19.4 us
    dot_general x8, matrix products, absorb(): jnp.dot(segment, table, preferred_element_type=jnp.float32)  8.12 us
    another operation x1, loops' own time, spectra_of(): lax.scan(absorb, start_total, jnp.arange(8, dtype=jnp.int32))  5.26 us
    dynamic_slice x8, local copies, waits for them, and re-layouts, spectra_of(): lax.scan(absorb, start_total, jnp.arange(8, dtype=jnp.int32))  5.19 us

commit v1 on v0

v1 whole, which is shorter than its diff:
```python
import functools
import math

import jax
import jax.numpy as jnp
import ml_dtypes
import numpy as np
from jax import lax
from jax.experimental import pallas as pl
from jax.experimental.pallas import tpu as pltpu
from jax.sharding import PartitionSpec as P

SAMPLES = 12000
FLO = 6
BINS = 595
HALF = 40
LAGS = 401
EPSILON = 1e-06

LANE = 128
BLOCKS = -(-BINS // LANE)
WIDTH = BLOCKS * LANE
CHUNK = 512
CHUNKS = -(-SAMPLES // CHUNK)
LAGS_PAD = 512

MESH = pl.DeviceIdType.MESH


def waves(steps):
    freq = FLO + np.arange(BINS, dtype=np.int64)
    angle = (steps[:, None] * freq[None, :] % SAMPLES) * (2.0 * math.pi / SAMPLES)
    pad = ((0, 0), (0, WIDTH - BINS))
    return np.pad(np.cos(angle), pad), np.pad(-np.sin(angle), pad)


def interleave(real_part, imag_part):
    rows = real_part.shape[0]
    both = np.stack(
        [real_part.reshape(rows, BLOCKS, LANE), imag_part.reshape(rows, BLOCKS, LANE)], axis=2
    )
    return both.reshape(rows, 2 * WIDTH)


def tables():
    dft = interleave(*waves(np.arange(CHUNK, dtype=np.int64))).astype(ml_dtypes.bfloat16)
    turn_real, turn_imag = waves(CHUNK * np.arange(CHUNKS, dtype=np.int64))
    turns = np.stack([turn_real, turn_imag]).astype(np.float32)
    spots = np.arange(WIDTH)
    inside = (spots[:, None] < BINS) & (spots[None, :] < BINS)
    near = (np.abs(spots[:, None] - spots[None, :]) <= HALF) & inside
    counts = np.maximum(near.sum(axis=0, keepdims=True), 1)
    band = near.astype(ml_dtypes.bfloat16)
    inverse = (1.0 / counts).astype(np.float32)
    lag_real, lag_imag = waves(np.arange(LAGS, dtype=np.int64) - (LAGS - 1) // 2)
    lag = np.pad(interleave(lag_real, lag_imag).T, ((0, 0), (0, LAGS_PAD - LAGS)))
    return dft, turns, band, inverse, lag.astype(ml_dtypes.bfloat16)


def spectrum_of(x_ref, dft_ref, turns_ref):
    pieces = []
    rows = x_ref.shape[0]
    for chunk in range(CHUNKS):
        first = chunk * CHUNK
        last = min(first + CHUNK, SAMPLES)
        piece = x_ref[:, first:last]
        if last - first < CHUNK:
            blank = jnp.zeros((rows, CHUNK - (last - first)), piece.dtype)
            piece = jnp.concatenate([piece, blank], axis=1)
        pieces.append(piece)
    signal = jnp.concatenate(pieces, axis=0)
    result = []
    for block in range(BLOCKS):
        lanes = slice(2 * LANE * block, 2 * LANE * (block + 1))
        part = jnp.dot(signal, dft_ref[:, lanes], preferred_element_type=jnp.float32)
        bins = slice(LANE * block, LANE * (block + 1))
        real_part = jnp.zeros((rows, LANE), jnp.float32)
        imag_part = jnp.zeros((rows, LANE), jnp.float32)
        for chunk in range(CHUNKS):
            own = part[rows * chunk : rows * (chunk + 1)]
            turn_real = turns_ref[0, chunk : chunk + 1, bins]
            turn_imag = turns_ref[1, chunk : chunk + 1, bins]
            real_part = real_part + (own[:, :LANE] * turn_real - own[:, LANE:] * turn_imag)
            imag_part = imag_part + (own[:, :LANE] * turn_imag + own[:, LANE:] * turn_real)
        result.append((real_part, imag_part))
    return result


def flag_column(mask_ref, rows):
    chans, segs = mask_ref.shape
    place = lax.broadcasted_iota(jnp.int32, (rows, LANE), 0)
    column = jnp.zeros((rows, LANE), jnp.float32)
    for seg in range(segs):
        for chan in range(chans):
            flag = mask_ref[chan, seg].astype(jnp.float32)
            column = jnp.where(place == seg * chans + chan, flag, column)
    return column


def whitened_blocks(mask_ref, x_ref, dft_ref, turns_ref, band_ref, inverse_ref):
    rows = x_ref.shape[0]
    spectrum = spectrum_of(x_ref, dft_ref, turns_ref)
    power = jnp.concatenate([re * re + im * im for re, im in spectrum], axis=1)
    high = power.astype(jnp.bfloat16)
    low = (power - high.astype(jnp.float32)).astype(jnp.bfloat16)
    sums = jnp.dot(
        jnp.concatenate([high, low], axis=0), band_ref[...], preferred_element_type=jnp.float32
    )
    smooth = (sums[:rows] + sums[rows:]) * inverse_ref[...]
    flags = flag_column(mask_ref, rows)
    scale = lax.rsqrt(smooth + EPSILON)
    result = []
    for block, (re, im) in enumerate(spectrum):
        factor = scale[:, LANE * block : LANE * (block + 1)] * flags
        real_part, imag_part = re * factor, im * factor
        if block == BLOCKS - 1:
            lane = lax.broadcasted_iota(jnp.int32, (rows, LANE), 1)
            real_part = jnp.where(lane == LANE - 1, flags, real_part)
        result.append((real_part, imag_part))
    return result


def exchange(
    panel_count, reach, mask_ref, x_ref, dft_ref, turns_ref, band_ref, inverse_ref,
    out_ref, send_sem, forward_sem, recv_sem,
):
    me = lax.axis_index("row")
    chips = panel_count // 2
    chip = me // 2
    core = lax.rem(me, 2)
    sibling = {"row": 2 * chip + 1 - core}

    def same_core(offset):
        return {"row": 2 * lax.rem(chip + offset + chips, chips) + core}

    barrier = pltpu.get_barrier_semaphore()
    for offset in range(1, chips):
        pl.semaphore_signal(barrier, inc=1, device_id=same_core(offset), device_id_type=MESH)
    pl.semaphore_signal(barrier, inc=1, device_id=sibling, device_id_type=MESH)

    blocks = whitened_blocks(mask_ref, x_ref, dft_ref, turns_ref, band_ref, inverse_ref)
    own = core + 1
    for block, (re, im) in enumerate(blocks):
        first = 2 * LANE * block
        out_ref[own, :, first : first + LANE] = re.astype(jnp.bfloat16)
        out_ref[own, :, first + LANE : first + 2 * LANE] = im.astype(jnp.bfloat16)

    pl.semaphore_wait(barrier, chips)

    def copy(source, target, sem, device):
        return pltpu.make_async_remote_copy(
            src_ref=out_ref.at[source],
            dst_ref=out_ref.at[target],
            send_sem=sem,
            recv_sem=recv_sem.at[target],
            device_id=device,
            device_id_type=MESH,
        )

    direct = [
        copy(own, 2 * step + core + 1, send_sem.at[step + 1], same_core(-step))
        for step in range(reach, 0, -1)
    ]
    back = copy(own, 0, send_sem.at[0], same_core(1))
    beside = copy(own, own, send_sem.at[1], sibling)
    for sent in direct:
        sent.start()

    @pl.when(core == 1)
    def _():
        back.start()

    beside.start()

    forwards = []
    back_forward = copy(0, 0, forward_sem.at[0], sibling)
    for step in range(1, reach + 1):
        slot = 2 * step + core + 1
        passed = copy(slot, slot, forward_sem.at[step], sibling)
        passed.wait_recv()
        passed.start()
        forwards.append(passed)
        if step == 1:

            @pl.when(core == 1)
            def _():
                back_forward.wait_recv()
                back_forward.start()

    copy(2 - core, 2 - core, send_sem.at[1], sibling).wait_recv()
    for step in range(1, reach + 1):
        slot = 2 * step + 2 - core
        copy(slot, slot, forward_sem.at[step], sibling).wait_recv()

    @pl.when(core == 0)
    def _():
        back_forward.wait_recv()

    for sent in direct + [beside] + forwards:
        sent.wait_send()

    @pl.when(core == 1)
    def _():
        back.wait_send()
        back_forward.wait_send()


def correlate(panel_count, pair_ref, panels_ref, lag_ref, stack_ref, out_ref, cross_ref):
    me = lax.axis_index("row")
    core = lax.rem(me, 2)
    first = me - core - 1
    step = pl.program_id(0)
    slots = stack_ref.shape[1]
    chans = stack_ref.shape[2]
    own = panels_ref[core + 1].astype(jnp.float32)
    segs = own.shape[0] // chans
    for slot in range(slots):
        panel = pair_ref[0, step * slots + slot]
        place = lax.rem(panel - first + panel_count, panel_count)
        partner = panels_ref[place].astype(jnp.float32)
        for chan in range(chans):
            scale = None
            for block in range(BLOCKS - 1, -1, -1):
                at = 2 * LANE * block
                re = im = 0.0
                for seg in range(segs):
                    mine = own[seg * chans + chan : seg * chans + chan + 1]
                    other = partner[seg * chans : (seg + 1) * chans]
                    own_re, own_im = mine[:, at : at + LANE], mine[:, at + LANE : at + 2 * LANE]
                    part_re, part_im = other[:, at : at + LANE], other[:, at + LANE : at + 2 * LANE]
                    re = re + (own_re * part_re + own_im * part_im)
                    im = im + (own_im * part_re - own_re * part_im)
                if scale is None:
                    count = re[:, LANE - 1 : LANE]
                    scale = 1.0 / jnp.maximum(count, 1.0)
                row = (slot * chans + chan) * chans
                cross_ref[row : row + chans, at : at + LANE] = (re * scale).astype(jnp.bfloat16)
                cross_ref[row : row + chans, at + LANE : at + 2 * LANE] = (im * scale).astype(
                    jnp.bfloat16
                )
    corr = jnp.dot(cross_ref[...], lag_ref[...], preferred_element_type=jnp.float32)
    corr = corr[:, :LAGS] * (1.0 / math.sqrt(BINS))
    out_ref[...] = stack_ref[...] + corr.reshape(stack_ref.shape)


def shards(traces, valid_mask, pair_table, stack_in):
    panel_count = lax.axis_size("row")
    chans, segs, samples = traces.shape
    rows = chans * segs
    offsets = pair_table.shape[1]
    reach = (offsets - 2) // 2
    dft, turns, band, inverse, lag = tables()
    x = jnp.transpose(traces, (1, 0, 2)).reshape(rows, samples)
    vmem = pl.BlockSpec(memory_space=pltpu.VMEM)
    smem = pl.BlockSpec(memory_space=pltpu.SMEM)
    panels = pl.pallas_call(
        functools.partial(exchange, panel_count, reach),
        out_shape=jax.ShapeDtypeStruct((offsets + 1, rows, 2 * WIDTH), jnp.bfloat16),
        in_specs=[smem] + [vmem] * 5,
        out_specs=vmem,
        scratch_shapes=[
            pltpu.SemaphoreType.DMA((reach + 2,)),
            pltpu.SemaphoreType.DMA((reach + 2,)),
            pltpu.SemaphoreType.DMA((offsets + 1,)),
        ],
        compiler_params=pltpu.CompilerParams(
            collective_id=0, has_side_effects=True, vmem_limit_bytes=32 << 20
        ),
    )(valid_mask, x, jnp.asarray(dft), jnp.asarray(turns), jnp.asarray(band), jnp.asarray(inverse))
    group = max(size for size in range(1, 7) if offsets % size == 0)
    tile = (1, group, chans, chans, stack_in.shape[4])
    return pl.pallas_call(
        functools.partial(correlate, panel_count),
        out_shape=jax.ShapeDtypeStruct(stack_in.shape, stack_in.dtype),
        grid_spec=pltpu.PrefetchScalarGridSpec(
            num_scalar_prefetch=1,
            grid=(offsets // group,),
            in_specs=[
                pl.BlockSpec(panels.shape, lambda i, pair: (0, 0, 0)),
                pl.BlockSpec(lag.shape, lambda i, pair: (0, 0)),
                pl.BlockSpec(tile, lambda i, pair: (0, i, 0, 0, 0)),
            ],
            out_specs=pl.BlockSpec(tile, lambda i, pair: (0, i, 0, 0, 0)),
            scratch_shapes=[pltpu.VMEM((group * chans * chans, 2 * WIDTH), jnp.bfloat16)],
        ),
        compiler_params=pltpu.CompilerParams(vmem_limit_bytes=32 << 20),
    )(pair_table, panels, jnp.asarray(lag), stack_in)


def solution(mesh):
    in_specs = (
        P(("parts", "row"), None, None),
        P(("parts", "row"), None),
        P(("parts", "row"), None),
        P(("parts", "row"), None, None, None, None),
    )
    out_specs = P(("parts", "row"), None, None, None, None)
    return jax.shard_map(shards, mesh=mesh, in_specs=in_specs, out_specs=out_specs, check_vma=False)
```

time: 215 us -> 21.2 us (0.10)
  other arithmetic: 143 us -> 0 us
  blocking collectives: 42.3 us -> 0 us
  Pallas kernels: 0 us -> 14.9 us
  matrix products: 11.3 us -> 0 us
  local copies, waits for them, and re-layouts: 12.1 us -> 5.84 us
  loops' own time: 5.26 us -> 0 us
    another operation x9 -> x0, other arithmetic: 138 us -> none
    all_gather x2 -> x0, blocking collectives: 42.3 us -> none  [the longest x1 23 us: shards(): lax.all_gather(own_flags, 'row', axis=0, tiled=True)]
    pallas_call x0 -> x2, Pallas kernels: none -> 14.9 us  [the longest x1 12 us: shards(): pl.pallas_call(functools.partial(exchange, panel_count, reach), out_shape...]
    dot_general x10 -> x0, matrix products: 11.3 us -> none  [the longest x8 8.12 us: absorb(): jnp.dot(segment, table, preferred_element_type=jnp.float32)]
    another operation x1 -> x0, loops' own time: 5.26 us -> none  [spectra_of(): lax.scan(absorb, start_total, jnp.arange(8, dtype=jnp.int32))]
    dynamic_slice x8 -> x0, local copies, waits for them, and re-layouts: 5.19 us -> none  [spectra_of(): lax.scan(absorb, start_total, jnp.arange(8, dtype=jnp.int32))]
    unnamed x6 -> x15, local copies, waits for them, and re-layouts: 0.08 us -> 4.8 us
    add x19 -> x0, other arithmetic: 2.27 us -> none  [the longest x1 1.44 us: shards(): base_stack + tile_corr(whitened, own_flags, partner, partner_flags, lag_t...]
where the time goes in v1:
time: 21.2 us; the launch traced here: 20.8 us
  Pallas kernels  14.9 us (70%)
  local copies, waits for them, and re-layouts  5.84 us (28%)
    pallas_call x1, Pallas kernels, shards(): pl.pallas_call(functools.partial(exchange, panel_count, reach), out_shape...  12 us
    unnamed x15, local copies, waits for them, and re-layouts  4.8 us
    pallas_call x1, Pallas kernels, shards(): pl.pallas_call(functools.partial(correlate, panel_count), out_shape=jax.S...  2.85 us
    transpose x1, local copies, waits for them, and re-layouts, shards(): x = jnp.transpose(traces, (1, 0, 2)).reshape(rows, samples)  1.03 us

profile of v1, /device:TPU:0, one launch (start us, length us, event | category | flops | bytes accessed | tf_op | source)
XLA Modules:
  0.0 20.8 jit_solution(9159766054890094784)
XLA Ops:
  0.0 0.8 %copy.11.mask_ref = s32[8,2]{1,0:T(8,128)S(1)} copy(s32[8,2]{0,1:T(2,128)} %param.10) | data formatting | bytes 128 | tf_op args[1]
  0.8 1.0 %copy.13 = bf16[2,8,12000]{2,1,0:T(8,128)(2,1)S(1)} copy(bf16[2,8,12000]{2,0,1:T(2,128)(2,1)} %bitcast.5) | data formatting | bytes 768000 | tf_op jit(solution)/shard_map/transpose | solution.py:253
  1.8 0.0 copy-start.2
  1.8 1.3 %copy-done.2 = bf16[512,1280]{1,0:T(8,128)(2,1)S(1)} copy-done((bf16[512,1280]{1,0:T(8,128)(2,1)S(1)}, bf16[512,1280]{1,0:T(8,128)(2,1)}, u32[]{:S(2)}) %copy-start.2) | copy-done | bytes 1310744
  3.1 0.0 copy-start.3
  3.1 1.1 %copy-done.3 = bf16[640,640]{1,0:T(8,128)(2,1)S(1)} copy-done((bf16[640,640]{1,0:T(8,128)(2,1)S(1)}, bf16[640,640]{1,0:T(8,128)(2,1)}, u32[]{:S(2)}) %copy-start.3) | copy-done | bytes 819224
  4.3 0.0 copy-start.4
  4.3 0.9 %copy-done.4 = f32[2,24,640]{2,1,0:T(8,128)S(1)} copy-done((f32[2,24,640]{2,1,0:T(8,128)S(1)}, f32[2,24,640]{2,1,0:T(8,128)}, u32[]{:S(2)}) %copy-start.4) | copy-done | bytes 122904
  5.2 0.0 copy-start.5
  5.2 0.7 %copy-done.5 = f32[1,640]{1,0:T(1,128)S(1)} copy-done((f32[1,640]{1,0:T(1,128)S(1)}, f32[1,640]{1,0:T(1,128)}, u32[]{:S(2)}) %copy-start.5) | copy-done | bytes 2584
  5.8 0.0 copy-start
  5.8 0.0 copy-start.1
  5.8 0.0 copy-start.6
  5.8 12.0 %shard_map.91.panels_ref = bf16[11,16,1280]{2,1,0:T(8,128)(2,1)S(1)} custom-call(s32[8,2]{1,0:T(8,128)S(1)} %copy.11.mask_ref, bf16[16,12000]{1,0:T(8,128)(2,1)S(1)} %bitcast.4, bf16[512,1280]{1,0:T(8,128)(2,1)S(1)} %copy-done.2, f32[2,24,640]{2,1,0:T(8,128)S(1)} %copy-done.4, bf16[640,640]{1,0:T(8,128)(2,1)S(1)} %copy-done.3, f32[1,640]{1,0:T(1,128)S(1)} %copy-done.5), custom_call_target="tpu_custom_call" | custom-call | tf_op jit(solution)/shard_map/pallas_call | solution.py:256
  17.9 0.0 copy-done
  17.9 0.0 copy-done.1
  17.9 0.0 copy-done.6
  17.9 2.9 %shard_map.92 = f32[1,10,8,8,401]{4,3,2,1,0:T(8,128)} custom-call(s32[1,10]{1,0:T(1,128)S(1)} %copy-done.6, bf16[11,16,1280]{2,1,0:T(8,128)(2,1)S(1)} %shard_map.91.panels_ref, bf16[1280,512]{1,0:T(8,128)(2,1)S(1)} %copy-done.1, f32[1,10,8,8,401]{4,3,2,1,0:T(8,128)S(1)} %copy-done), custom_call_target="tpu_custom_call" | custom-call | tf_op jit(solution)/shard_map/pallas_call | solution.py:272
Async XLA Ops:
  1.8 1.3 %copy-start.2 = (bf16[512,1280]{1,0:T(8,128)(2,1)S(1)}, bf16[512,1280]{1,0:T(8,128)(2,1)}, u32[]{:S(2)}) copy-start(bf16[512,1280]{1,0:T(8,128)(2,1)} %constant.10.clone.dft_ref) | copy-start | bytes 3932164
  3.1 1.1 %copy-start.3 = (bf16[640,640]{1,0:T(8,128)(2,1)S(1)}, bf16[640,640]{1,0:T(8,128)(2,1)}, u32[]{:S(2)}) copy-start(bf16[640,640]{1,0:T(8,128)(2,1)} %constant.12.clone.band_ref) | copy-start | bytes 2457604
  4.3 0.9 %copy-start.4 = (f32[2,24,640]{2,1,0:T(8,128)S(1)}, f32[2,24,640]{2,1,0:T(8,128)}, u32[]{:S(2)}) copy-start(f32[2,24,640]{2,1,0:T(8,128)} %constant.11.clone.turns_ref) | copy-start | bytes 368644
  5.2 0.7 %copy-start.5 = (f32[1,640]{1,0:T(1,128)S(1)}, f32[1,640]{1,0:T(1,128)}, u32[]{:S(2)}) copy-start(f32[1,640]{1,0:T(1,128)} %constant.13.clone.inverse_ref) | copy-start | bytes 7684
  5.8 12.0 %copy-start = (f32[1,10,8,8,401]{4,3,2,1,0:T(8,128)S(1)}, f32[1,10,8,8,401]{4,3,2,1,0:T(8,128)}, u32[]{:S(2)}) copy-start(f32[1,10,8,8,401]{4,3,2,1,0:T(8,128)} %stack_ref.1) | copy-start | bytes 3079684
  5.8 12.1 %copy-start.1 = (bf16[1280,512]{1,0:T(8,128)(2,1)S(1)}, bf16[1280,512]{1,0:T(8,128)(2,1)}, u32[]{:S(2)}) copy-start(bf16[1280,512]{1,0:T(8,128)(2,1)} %constant.14.clone.lag_ref) | copy-start | bytes 3932164
  5.8 12.1 %copy-start.6 = (s32[1,10]{1,0:T(1,128)S(1)}, s32[1,10]{1,0:T(1,128)}, u32[]{:S(2)}) copy-start(s32[1,10]{1,0:T(1,128)} %pair_ref.1) | copy-start | bytes 124

commit v2 on v1

v2 whole, which is shorter than its diff:
```python
import functools
import math

import jax
import jax.numpy as jnp
import ml_dtypes
import numpy as np
from jax import lax
from jax.experimental import pallas as pl
from jax.experimental.pallas import tpu as pltpu
from jax.sharding import PartitionSpec as P

SAMPLES = 12000
FLO = 6
BINS = 595
HALF = 40
LAGS = 401
EPSILON = 1e-06

LANE = 128
BLOCKS = -(-BINS // LANE)
WIDTH = BLOCKS * LANE
CHUNK = 512
CHUNKS = -(-SAMPLES // CHUNK)
LAGS_PAD = 512

MESH = pl.DeviceIdType.MESH


def waves(steps):
    freq = FLO + np.arange(BINS, dtype=np.int64)
    angle = (steps[:, None] * freq[None, :] % SAMPLES) * (2.0 * math.pi / SAMPLES)
    pad = ((0, 0), (0, WIDTH - BINS))
    return np.pad(np.cos(angle), pad), np.pad(-np.sin(angle), pad)


def interleave(real_part, imag_part):
    rows = real_part.shape[0]
    both = np.stack(
        [real_part.reshape(rows, BLOCKS, LANE), imag_part.reshape(rows, BLOCKS, LANE)], axis=2
    )
    return both.reshape(rows, 2 * WIDTH)


def tables():
    dft = interleave(*waves(np.arange(CHUNK, dtype=np.int64))).astype(ml_dtypes.bfloat16)
    turn_real, turn_imag = waves(CHUNK * np.arange(CHUNKS, dtype=np.int64))
    spots = np.arange(WIDTH)
    inside = (spots[:, None] < BINS) & (spots[None, :] < BINS)
    near = (np.abs(spots[:, None] - spots[None, :]) <= HALF) & inside
    counts = np.maximum(near.sum(axis=0, keepdims=True), 1)
    band = near.astype(ml_dtypes.bfloat16)
    turns = np.concatenate([turn_real, turn_imag, 1.0 / counts], axis=0)
    turns = np.pad(turns, ((0, -turns.shape[0] % 8), (0, 0))).astype(np.float32)
    lag_real, lag_imag = waves(np.arange(LAGS, dtype=np.int64) - (LAGS - 1) // 2)
    lag = np.pad(interleave(lag_real, lag_imag).T, ((0, 0), (0, LAGS_PAD - LAGS)))
    return dft, turns, band, lag.astype(ml_dtypes.bfloat16)


def spectrum_of(x_ref, dft_ref, turns_ref, ready):
    pieces = []
    chans, segs = x_ref.shape[:2]
    rows = chans * segs
    for chunk in range(CHUNKS):
        first = chunk * CHUNK
        last = min(first + CHUNK, SAMPLES)
        piece = x_ref[:, :, first:last].reshape(rows, last - first)
        if last - first < CHUNK:
            blank = jnp.zeros((rows, CHUNK - (last - first)), piece.dtype)
            piece = jnp.concatenate([piece, blank], axis=1)
        pieces.append(piece)
    signal = jnp.concatenate(pieces, axis=0)
    result = []
    for block in range(BLOCKS):
        ready(block)
        lanes = slice(2 * LANE * block, 2 * LANE * (block + 1))
        part = jnp.dot(signal, dft_ref[:, lanes], preferred_element_type=jnp.float32)
        bins = slice(LANE * block, LANE * (block + 1))
        real_part = jnp.zeros((rows, LANE), jnp.float32)
        imag_part = jnp.zeros((rows, LANE), jnp.float32)
        for chunk in range(CHUNKS):
            own = part[rows * chunk : rows * (chunk + 1)]
            turn_real = turns_ref[chunk : chunk + 1, bins]
            turn_imag = turns_ref[CHUNKS + chunk : CHUNKS + chunk + 1, bins]
            real_part = real_part + (own[:, :LANE] * turn_real - own[:, LANE:] * turn_imag)
            imag_part = imag_part + (own[:, :LANE] * turn_imag + own[:, LANE:] * turn_real)
        result.append((real_part, imag_part))
    return result


def flag_column(mask_ref, rows):
    segs, chans = mask_ref.shape
    place = lax.broadcasted_iota(jnp.int32, (rows, LANE), 0)
    column = jnp.zeros((rows, LANE), jnp.float32)
    for seg in range(segs):
        for chan in range(chans):
            flag = mask_ref[seg, chan].astype(jnp.float32)
            column = jnp.where(place == chan * segs + seg, flag, column)
    return column


def whitened_blocks(mask_ref, x_ref, dft_ref, turns_ref, band_ref, ready, band_ready):
    rows = x_ref.shape[0] * x_ref.shape[1]
    spectrum = spectrum_of(x_ref, dft_ref, turns_ref, ready)
    band_ready()
    power = jnp.concatenate([re * re + im * im for re, im in spectrum], axis=1)
    high = power.astype(jnp.bfloat16)
    low = (power - high.astype(jnp.float32)).astype(jnp.bfloat16)
    sums = jnp.dot(
        jnp.concatenate([high, low], axis=0), band_ref[...], preferred_element_type=jnp.float32
    )
    smooth = (sums[:rows] + sums[rows:]) * turns_ref[2 * CHUNKS : 2 * CHUNKS + 1]
    flags = flag_column(mask_ref, rows)
    scale = lax.rsqrt(smooth + EPSILON)
    result = []
    for block, (re, im) in enumerate(spectrum):
        factor = scale[:, LANE * block : LANE * (block + 1)] * flags
        real_part, imag_part = re * factor, im * factor
        if block == BLOCKS - 1:
            lane = lax.broadcasted_iota(jnp.int32, (rows, LANE), 1)
            real_part = jnp.where(lane == LANE - 1, flags, real_part)
        result.append((real_part, imag_part))
    return result


def kernel(
    panel_count, mask_ref, pair_ref, x_hbm, dft_hbm, turns_hbm, band_hbm, lag_hbm, stack_hbm,
    out_ref, x_ref, dft_ref, turns_ref, band_ref, lag_ref, stack_ref, white_ref, panels_ref,
    cross_ref, corr_ref, load_sem, send_sem, forward_sem, recv_sem,
):
    offsets, chans = stack_ref.shape[:2]
    segs = x_ref.shape[1]
    reach = (offsets - 2) // 2
    loads = [
        pltpu.make_async_copy(x_hbm, x_ref, load_sem.at[0]),
        pltpu.make_async_copy(turns_hbm, turns_ref, load_sem.at[1]),
    ]
    for block in range(BLOCKS):
        lanes = pl.ds(2 * LANE * block, 2 * LANE)
        loads.append(
            pltpu.make_async_copy(
                dft_hbm.at[:, lanes], dft_ref.at[:, lanes], load_sem.at[2 + block]
            )
        )
    loads.append(pltpu.make_async_copy(band_hbm, band_ref, load_sem.at[2 + BLOCKS]))
    late_loads = [
        pltpu.make_async_copy(lag_hbm, lag_ref, load_sem.at[3 + BLOCKS]),
        pltpu.make_async_copy(stack_hbm.at[0], stack_ref, load_sem.at[4 + BLOCKS]),
    ]
    for load in loads + late_loads:
        load.start()

    me = lax.axis_index("row")
    chips = panel_count // 2
    chip = me // 2
    core = lax.rem(me, 2)
    sibling = {"row": 2 * chip + 1 - core}

    def same_core(offset):
        return {"row": 2 * lax.rem(chip + offset + chips, chips) + core}

    barrier = pltpu.get_barrier_semaphore()
    for offset in range(1, chips):
        pl.semaphore_signal(barrier, inc=1, device_id=same_core(offset), device_id_type=MESH)
    pl.semaphore_signal(barrier, inc=1, device_id=sibling, device_id_type=MESH)

    loads[0].wait()
    loads[1].wait()
    blocks = whitened_blocks(
        mask_ref, x_ref, dft_ref, turns_ref, band_ref,
        lambda block: loads[2 + block].wait(), loads[2 + BLOCKS].wait,
    )
    own = core + 1
    for place, part in enumerate(part for pair in blocks for part in pair):
        white_ref[place] = part
        ordered = [white_ref[place, pl.ds(seg, chans, stride=segs), :] for seg in range(segs)]
        panels_ref[own, :, LANE * place : LANE * (place + 1)] = jnp.concatenate(
            ordered, axis=0
        ).astype(jnp.bfloat16)

    pl.semaphore_wait(barrier, chips)

    def copy(source, target, sem, device):
        return pltpu.make_async_remote_copy(
            src_ref=panels_ref.at[source],
            dst_ref=panels_ref.at[target],
            send_sem=sem,
            recv_sem=recv_sem.at[target],
            device_id=device,
            device_id_type=MESH,
        )

    direct = [
        copy(own, 2 * step + core + 1, send_sem.at[step + 1], same_core(-step))
        for step in range(1, reach + 1)
    ]
    back = copy(own, 0, send_sem.at[0], same_core(1))
    beside = copy(own, own, send_sem.at[1], sibling)
    beside.start()
    for sent in direct:
        sent.start()

    @pl.when(core == 1)
    def _():
        back.start()

    def correlate(slots):
        mine = panels_ref[own].astype(jnp.float32)
        for index, slot in enumerate(slots):
            partner = panels_ref[slot].astype(jnp.float32)
            scales = [None] * chans
            for block in range(BLOCKS - 1, -1, -1):
                at = 2 * LANE * block
                cut_re, cut_im = slice(at, at + LANE), slice(at + LANE, at + 2 * LANE)
                real_rows, imag_rows = [], []
                for chan in range(chans):
                    re = im = 0.0
                    for seg in range(segs):
                        row = slice(seg * chans + chan, seg * chans + chan + 1)
                        other = slice(seg * chans, (seg + 1) * chans)
                        own_re, own_im = mine[row, cut_re], mine[row, cut_im]
                        part_re, part_im = partner[other, cut_re], partner[other, cut_im]
                        re = re + (own_re * part_re + own_im * part_im)
                        im = im + (own_im * part_re - own_re * part_im)
                    if scales[chan] is None:
                        scales[chan] = 1.0 / jnp.maximum(re[:, LANE - 1 : LANE], 1.0)
                    real_rows.append(re * scales[chan])
                    imag_rows.append(im * scales[chan])
                rows = slice(index * chans * chans, (index + 1) * chans * chans)
                cross_ref[rows, cut_re] = jnp.concatenate(real_rows, axis=0).astype(jnp.bfloat16)
                cross_ref[rows, cut_im] = jnp.concatenate(imag_rows, axis=0).astype(jnp.bfloat16)
        corr = jnp.dot(cross_ref[...], lag_ref[...], preferred_element_type=jnp.float32)
        corr = corr[:, :LAGS] * (1.0 / math.sqrt(BINS))
        for index, slot in enumerate(slots):
            corr_ref[slot] = corr[index * chans * chans : (index + 1) * chans * chans]

    copy(2 - core, 2 - core, send_sem.at[1], sibling).wait_recv()
    for load in late_loads:
        load.wait()
    correlate([1, 2])

    def forward(slot, step):
        return copy(slot, slot, forward_sem.at[step], sibling)

    def arrive(step, carry):
        passed = forward(2 * step + core + 1, step)
        passed.wait_recv()
        passed.start()
        forward(2 * step + 2 - core, step).wait_recv()
        correlate([2 * step + 1, 2 * step + 2])
        return carry

    lax.fori_loop(1, reach, arrive, 0)

    far = 2 * reach + 1
    passed = forward(far * (1 - core), reach)
    passed.wait_recv()
    passed.start()

    @pl.when(core == 1)
    def _():
        copy(far + 1, far + 1, send_sem.at[0], sibling).wait_recv()

    forward(far * core, reach).wait_recv()
    correlate([far, (far + 1) * core])

    first = me - core - 1

    def accumulate(slot, carry):
        place = lax.rem(pair_ref[0, slot] - first + panel_count, panel_count)
        place = jnp.clip(place, 0, offsets)
        out_ref[0, slot] = stack_ref[slot] + corr_ref[place].reshape(stack_ref.shape[1:])
        return carry

    lax.fori_loop(0, offsets, accumulate, 0, unroll=2)

    for sent in direct + [beside]:
        sent.wait_send()

    def forwarded(step, carry):
        forward(own, step).wait_send()
        return carry

    lax.fori_loop(1, reach + 1, forwarded, 0)

    @pl.when(core == 1)
    def _():
        back.wait_send()


def shards(traces, valid_mask, pair_table, stack_in):
    panel_count = lax.axis_size("row")
    chans, segs, samples = traces.shape
    rows = chans * segs
    offsets = pair_table.shape[1]
    reach = (offsets - 2) // 2
    dft, turns, band, lag = tables()
    vmem = pl.BlockSpec(memory_space=pltpu.VMEM)
    hbm = pl.BlockSpec(memory_space=pltpu.HBM)
    smem = pl.BlockSpec(memory_space=pltpu.SMEM)
    return pl.pallas_call(
        functools.partial(kernel, panel_count),
        out_shape=jax.ShapeDtypeStruct(stack_in.shape, stack_in.dtype),
        in_specs=[smem] * 2 + [hbm] * 6,
        out_specs=vmem,
        scratch_shapes=[
            pltpu.VMEM(traces.shape, traces.dtype),
            pltpu.VMEM(dft.shape, jnp.bfloat16),
            pltpu.VMEM(turns.shape, jnp.float32),
            pltpu.VMEM(band.shape, jnp.bfloat16),
            pltpu.VMEM(lag.shape, jnp.bfloat16),
            pltpu.VMEM(stack_in.shape[1:], jnp.float32),
            pltpu.VMEM((2 * BLOCKS, rows, LANE), jnp.float32),
            pltpu.VMEM((offsets + 1, rows, 2 * WIDTH), jnp.bfloat16),
            pltpu.VMEM((2 * chans * chans, 2 * WIDTH), jnp.bfloat16),
            pltpu.VMEM((offsets + 1, chans * chans, LAGS), jnp.float32),
            pltpu.SemaphoreType.DMA((5 + BLOCKS,)),
            pltpu.SemaphoreType.DMA((reach + 2,)),
            pltpu.SemaphoreType.DMA((reach + 1,)),
            pltpu.SemaphoreType.DMA((offsets + 1,)),
        ],
        compiler_params=pltpu.CompilerParams(
            collective_id=0, has_side_effects=True, vmem_limit_bytes=56 << 20
        ),
    )(
        valid_mask.T, pair_table, traces, jnp.asarray(dft), jnp.asarray(turns),
        jnp.asarray(band), jnp.asarray(lag), stack_in,
    )


def solution(mesh):
    in_specs = (
        P(("parts", "row"), None, None),
        P(("parts", "row"), None),
        P(("parts", "row"), None),
        P(("parts", "row"), None, None, None, None),
    )
    out_specs = P(("parts", "row"), None, None, None, None)
    return jax.shard_map(shards, mesh=mesh, in_specs=in_specs, out_specs=out_specs, check_vma=False)
```

time: 21.2 us -> 19.9 us (0.939); the launches traced: 20.8 us -> 19.7 us
  local copies, waits for them, and re-layouts: 5.84 us -> 2.47 us
  Pallas kernels: 14.9 us -> 17.3 us
    pallas_call x2 -> x1, Pallas kernels: 14.9 us -> 17.3 us  [shards(): pl.pallas_call(functools.partial(kernel, panel_count), out_shape=jax.Shap...]
    unnamed x15 -> x1, local copies, waits for them, and re-layouts: 4.8 us -> 2.47 us
    transpose x1 -> x0, local copies, waits for them, and re-layouts: 1.03 us -> none  [shards(): x = jnp.transpose(traces, (1, 0, 2)).reshape(rows, samples)]
where the time goes in v2:
time: 19.9 us; the launch traced here: 19.7 us
  Pallas kernels  17.3 us (87%)
  local copies, waits for them, and re-layouts  2.47 us (12%)
    pallas_call x1, Pallas kernels, shards(): pl.pallas_call(functools.partial(kernel, panel_count), out_shape=jax.Shap...  17.3 us
    unnamed x1, local copies, waits for them, and re-layouts  2.47 us

profile of v2, /device:TPU:0, one launch (start us, length us, event | category | flops | bytes accessed | tf_op | source)
XLA Modules:
  0.0 19.7 jit_solution(838211834658221726)
XLA Ops:
  0.0 17.3 %shard_map.82 = f32[1,10,8,8,401]{4,3,2,1,0:T(8,128)} custom-call(s32[2,8]{1,0:T(2,128)} %bitcast.1, s32[1,10]{1,0:T(1,128)} %pair_ref.1, bf16[8,2,12000]{2,1,0:T(2,128)(2,1)} %x_hbm.1, bf16[512,1280]{1,0:T(8,128)(2,1)} %constant.8.clone.dft_hbm, f32[56,640]{1,0:T(8,128)} %constant.9.clone.turns_hbm, bf16[640,640]{1,0:T(8,128)(2,1)} %constant.10.clone.band_hbm, ...), custom_call_target="tpu_custom_call" | custom-call | tf_op jit(solution)/shard_map/pallas_call | solution.py:301
  17.3 2.5 %copy.10 = f32[1,10,8,8,401]{4,3,2,1,0:T(8,128)} copy(f32[1,10,8,8,401]{4,3,2,1,0:T(8,128)} %shard_map.82) | data formatting | bytes 2053120

commit v3 on v2

--- a/solution.py
+++ b/solution.py
@@ -123,14 +123,11 @@
     return result
 
 
-def kernel(
-    panel_count, mask_ref, pair_ref, x_hbm, dft_hbm, turns_hbm, band_hbm, lag_hbm, stack_hbm,
-    out_ref, x_ref, dft_ref, turns_ref, band_ref, lag_ref, stack_ref, white_ref, panels_ref,
-    cross_ref, corr_ref, load_sem, send_sem, forward_sem, recv_sem,
+def exchange(
+    panel_count, reach, mask_ref, x_hbm, dft_hbm, turns_hbm, band_hbm,
+    out_ref, x_ref, dft_ref, turns_ref, band_ref, white_ref, load_sem,
+    send_sem, forward_sem, recv_sem,
 ):
-    offsets, chans = stack_ref.shape[:2]
-    segs = x_ref.shape[1]
-    reach = (offsets - 2) // 2
     loads = [
         pltpu.make_async_copy(x_hbm, x_ref, load_sem.at[0]),
         pltpu.make_async_copy(turns_hbm, turns_ref, load_sem.at[1]),
@@ -143,11 +140,7 @@
             )
         )
     loads.append(pltpu.make_async_copy(band_hbm, band_ref, load_sem.at[2 + BLOCKS]))
-    late_loads = [
-        pltpu.make_async_copy(lag_hbm, lag_ref, load_sem.at[3 + BLOCKS]),
-        pltpu.make_async_copy(stack_hbm.at[0], stack_ref, load_sem.at[4 + BLOCKS]),
-    ]
-    for load in loads + late_loads:
+    for load in loads:
         load.start()
 
     me = lax.axis_index("row")
@@ -171,10 +164,11 @@
         lambda block: loads[2 + block].wait(), loads[2 + BLOCKS].wait,
     )
     own = core + 1
+    chans, segs = x_ref.shape[:2]
     for place, part in enumerate(part for pair in blocks for part in pair):
         white_ref[place] = part
         ordered = [white_ref[place, pl.ds(seg, chans, stride=segs), :] for seg in range(segs)]
-        panels_ref[own, :, LANE * place : LANE * (place + 1)] = jnp.concatenate(
+        out_ref[own, :, LANE * place : LANE * (place + 1)] = jnp.concatenate(
             ordered, axis=0
         ).astype(jnp.bfloat16)
 
@@ -182,8 +176,8 @@
 
     def copy(source, target, sem, device):
         return pltpu.make_async_remote_copy(
-            src_ref=panels_ref.at[source],
-            dst_ref=panels_ref.at[target],
+            src_ref=out_ref.at[source],
+            dst_ref=out_ref.at[target],
             send_sem=sem,
             recv_sem=recv_sem.at[target],
             device_id=device,
@@ -192,11 +186,10 @@
 
     direct = [
         copy(own, 2 * step + core + 1, send_sem.at[step + 1], same_core(-step))
-        for step in range(1, reach + 1)
+        for step in range(reach, 0, -1)
     ]
     back = copy(own, 0, send_sem.at[0], same_core(1))
     beside = copy(own, own, send_sem.at[1], sibling)
-    beside.start()
     for sent in direct:
         sent.start()
 
@@ -204,10 +197,71 @@
     def _():
         back.start()
 
-    def correlate(slots):
-        mine = panels_ref[own].astype(jnp.float32)
-        for index, slot in enumerate(slots):
-            partner = panels_ref[slot].astype(jnp.float32)
+    beside.start()
+
+    forwards = []
+    back_forward = copy(0, 0, forward_sem.at[0], sibling)
+    for step in range(1, reach + 1):
+        slot = 2 * step + core + 1
+        passed = copy(slot, slot, forward_sem.at[step], sibling)
+        passed.wait_recv()
+        passed.start()
+        forwards.append(passed)
+        if step == 1:
+
+            @pl.when(core == 1)
+            def _():
+                back_forward.wait_recv()
+                back_forward.start()
+
+    copy(2 - core, 2 - core, send_sem.at[1], sibling).wait_recv()
+    for step in range(1, reach + 1):
+        slot = 2 * step + 2 - core
+        copy(slot, slot, forward_sem.at[step], sibling).wait_recv()
+
+    @pl.when(core == 0)
+    def _():
+        back_forward.wait_recv()
+
+    for sent in direct + [beside] + forwards:
+        sent.wait_send()
+
+    @pl.when(core == 1)
+    def _():
+        back.wait_send()
+        back_forward.wait_send()
+
+
+def correlate(
+    panel_count, group, pair_ref, panels_hbm, lag_hbm, stack_hbm, out_hbm,
+    panels_ref, lag_ref, stack_ref, cross_ref, load_sem, out_sem,
+):
+    offsets, chans = stack_ref.shape[:2]
+    loads = [
+        pltpu.make_async_copy(panels_hbm, panels_ref, load_sem.at[0]),
+        pltpu.make_async_copy(lag_hbm, lag_ref, load_sem.at[1]),
+        pltpu.make_async_copy(stack_hbm.at[0], stack_ref, load_sem.at[2]),
+    ]
+    for load in loads:
+        load.start()
+    me = lax.axis_index("row")
+    core = lax.rem(me, 2)
+    first = me - core - 1
+    loads[0].wait()
+    own = panels_ref[core + 1].astype(jnp.float32)
+    segs = own.shape[0] // chans
+
+    def result(step):
+        slots = pl.ds(step * group, group)
+        return pltpu.make_async_copy(
+            stack_ref.at[slots], out_hbm.at[0, slots], out_sem.at[step]
+        )
+
+    def advance(step, carry):
+        for slot in range(group):
+            panel = pair_ref[0, step * group + slot]
+            place = lax.rem(panel - first + panel_count, panel_count)
+            partner = panels_ref[jnp.clip(place, 0, offsets)].astype(jnp.float32)
             scales = [None] * chans
             for block in range(BLOCKS - 1, -1, -1):
                 at = 2 * LANE * block
@@ -218,7 +272,7 @@
                     for seg in range(segs):
                         row = slice(seg * chans + chan, seg * chans + chan + 1)
                         other = slice(seg * chans, (seg + 1) * chans)
-                        own_re, own_im = mine[row, cut_re], mine[row, cut_im]
+                        own_re, own_im = own[row, cut_re], own[row, cut_im]
                         part_re, part_im = partner[other, cut_re], partner[other, cut_im]
                         re = re + (own_re * part_re + own_im * part_im)
                         im = im + (own_im * part_re - own_re * part_im)
@@ -226,66 +280,29 @@
                         scales[chan] = 1.0 / jnp.maximum(re[:, LANE - 1 : LANE], 1.0)
                     real_rows.append(re * scales[chan])
                     imag_rows.append(im * scales[chan])
-                rows = slice(index * chans * chans, (index + 1) * chans * chans)
+                rows = slice(slot * chans * chans, (slot + 1) * chans * chans)
                 cross_ref[rows, cut_re] = jnp.concatenate(real_rows, axis=0).astype(jnp.bfloat16)
                 cross_ref[rows, cut_im] = jnp.concatenate(imag_rows, axis=0).astype(jnp.bfloat16)
+
+        @pl.when(step == 0)
+        def _():
+            loads[1].wait()
+            loads[2].wait()
+
         corr = jnp.dot(cross_ref[...], lag_ref[...], preferred_element_type=jnp.float32)
         corr = corr[:, :LAGS] * (1.0 / math.sqrt(BINS))
-        for index, slot in enumerate(slots):
-            corr_ref[slot] = corr[index * chans * chans : (index + 1) * chans * chans]
-
-    copy(2 - core, 2 - core, send_sem.at[1], sibling).wait_recv()
-    for load in late_loads:
-        load.wait()
-    correlate([1, 2])
-
-    def forward(slot, step):
-        return copy(slot, slot, forward_sem.at[step], sibling)
-
-    def arrive(step, carry):
-        passed = forward(2 * step + core + 1, step)
-        passed.wait_recv()
-        passed.start()
-        forward(2 * step + 2 - core, step).wait_recv()
-        correlate([2 * step + 1, 2 * step + 2])
+        slots = pl.ds(step * group, group)
+        stack_ref[slots] = stack_ref[slots] + corr.reshape((group,) + stack_ref.shape[1:])
+        result(step).start()
         return carry
 
-    lax.fori_loop(1, reach, arrive, 0)
-
-    far = 2 * reach + 1
-    passed = forward(far * (1 - core), reach)
-    passed.wait_recv()
-    passed.start()
-
-    @pl.when(core == 1)
-    def _():
-        copy(far + 1, far + 1, send_sem.at[0], sibling).wait_recv()
-
-    forward(far * core, reach).wait_recv()
-    correlate([far, (far + 1) * core])
-
-    first = me - core - 1
-
-    def accumulate(slot, carry):
-        place = lax.rem(pair_ref[0, slot] - first + panel_count, panel_count)
-        place = jnp.clip(place, 0, offsets)
-        out_ref[0, slot] = stack_ref[slot] + corr_ref[place].reshape(stack_ref.shape[1:])
+    lax.fori_loop(0, offsets // group, advance, 0)
+
+    def finish(step, carry):
+        result(step).wait()
         return carry
 
-    lax.fori_loop(0, offsets, accumulate, 0, unroll=2)
-
-    for sent in direct + [beside]:
-        sent.wait_send()
-
-    def forwarded(step, carry):
-        forward(own, step).wait_send()
-        return carry
-
-    lax.fori_loop(1, reach + 1, forwarded, 0)
-
-    @pl.when(core == 1)
-    def _():
-        back.wait_send()
+    lax.fori_loop(0, offsets // group, finish, 0)
 
 
 def shards(traces, valid_mask, pair_table, stack_in):
@@ -298,34 +315,42 @@
     vmem = pl.BlockSpec(memory_space=pltpu.VMEM)
     hbm = pl.BlockSpec(memory_space=pltpu.HBM)
     smem = pl.BlockSpec(memory_space=pltpu.SMEM)
-    return pl.pallas_call(
-        functools.partial(kernel, panel_count),
-        out_shape=jax.ShapeDtypeStruct(stack_in.shape, stack_in.dtype),
-        in_specs=[smem] * 2 + [hbm] * 6,
+    panels = pl.pallas_call(
+        functools.partial(exchange, panel_count, reach),
+        out_shape=jax.ShapeDtypeStruct((offsets + 1, rows, 2 * WIDTH), jnp.bfloat16),
+        in_specs=[smem] + [hbm] * 4,
         out_specs=vmem,
         scratch_shapes=[
             pltpu.VMEM(traces.shape, traces.dtype),
             pltpu.VMEM(dft.shape, jnp.bfloat16),
             pltpu.VMEM(turns.shape, jnp.float32),
             pltpu.VMEM(band.shape, jnp.bfloat16),
-            pltpu.VMEM(lag.shape, jnp.bfloat16),
-            pltpu.VMEM(stack_in.shape[1:], jnp.float32),
             pltpu.VMEM((2 * BLOCKS, rows, LANE), jnp.float32),
-            pltpu.VMEM((offsets + 1, rows, 2 * WIDTH), jnp.bfloat16),
-            pltpu.VMEM((2 * chans * chans, 2 * WIDTH), jnp.bfloat16),
-            pltpu.VMEM((offsets + 1, chans * chans, LAGS), jnp.float32),
-            pltpu.SemaphoreType.DMA((5 + BLOCKS,)),
+            pltpu.SemaphoreType.DMA((3 + BLOCKS,)),
             pltpu.SemaphoreType.DMA((reach + 2,)),
-            pltpu.SemaphoreType.DMA((reach + 1,)),
+            pltpu.SemaphoreType.DMA((reach + 2,)),
             pltpu.SemaphoreType.DMA((offsets + 1,)),
         ],
         compiler_params=pltpu.CompilerParams(
-            collective_id=0, has_side_effects=True, vmem_limit_bytes=56 << 20
+            collective_id=0, has_side_effects=True, vmem_limit_bytes=60 << 20
         ),
-    )(
-        valid_mask.T, pair_table, traces, jnp.asarray(dft), jnp.asarray(turns),
-        jnp.asarray(band), jnp.asarray(lag), stack_in,
-    )
+    )(valid_mask.T, traces, jnp.asarray(dft), jnp.asarray(turns), jnp.asarray(band))
+    group = max(size for size in range(1, 7) if offsets % size == 0)
+    return pl.pallas_call(
+        functools.partial(correlate, panel_count, group),
+        out_shape=jax.ShapeDtypeStruct(stack_in.shape, stack_in.dtype),
+        in_specs=[smem] + [hbm] * 3,
+        out_specs=hbm,
+        scratch_shapes=[
+            pltpu.VMEM(panels.shape, panels.dtype),
+            pltpu.VMEM(lag.shape, jnp.bfloat16),
+            pltpu.VMEM(stack_in.shape[1:], jnp.float32),
+            pltpu.VMEM((group * chans * chans, 2 * WIDTH), jnp.bfloat16),
+            pltpu.SemaphoreType.DMA((3,)),
+            pltpu.SemaphoreType.DMA((offsets // group,)),
+        ],
+        compiler_params=pltpu.CompilerParams(vmem_limit_bytes=56 << 20),
+    )(pair_table, panels, jnp.asarray(lag), stack_in)
 
 
 def solution(mesh):

time: 19.9 us -> 20.4 us (1.025)
  Pallas kernels: 17.3 us -> 20.2 us
  local copies, waits for them, and re-layouts: 2.47 us -> 0 us
    pallas_call x1 -> x2, Pallas kernels: 17.3 us -> 20.2 us  [the longest x1 15.1 us: shards(): pl.pallas_call(functools.partial(exchange, panel_count, reach), out_shape...]
    unnamed x1 -> x0, local copies, waits for them, and re-layouts: 2.47 us -> none
where the time goes in v3:
time: 20.4 us; the launch traced here: 20.2 us
  Pallas kernels  20.2 us (99%)
    pallas_call x1, Pallas kernels, shards(): pl.pallas_call(functools.partial(exchange, panel_count, reach), out_shape...  15.1 us
    pallas_call x1, Pallas kernels, shards(): pl.pallas_call(functools.partial(correlate, panel_count, group), out_shap...  5.13 us

profile of v3, /device:TPU:0, one launch (start us, length us, event | category | flops | bytes accessed | tf_op | source)
XLA Modules:
  0.0 20.2 jit_solution(12706852509339856552)
XLA Ops:
  0.0 15.1 %shard_map.82.panels_hbm = bf16[11,16,1280]{2,1,0:T(8,128)(2,1)} custom-call(s32[2,8]{1,0:T(2,128)} %bitcast.1, bf16[8,2,12000]{2,1,0:T(2,128)(2,1)} %x_hbm.1, bf16[512,1280]{1,0:T(8,128)(2,1)} %constant.8.clone.dft_hbm, f32[56,640]{1,0:T(8,128)} %constant.9.clone.turns_hbm, bf16[640,640]{1,0:T(8,128)(2,1)} %constant.10.clone.band_hbm), custom_call_target="tpu_custom_call" | custom-call | tf_op jit(solution)/shard_map/pallas_call | solution.py:318
  15.1 5.1 %shard_map.83 = f32[1,10,8,8,401]{4,3,2,1,0:T(8,128)} custom-call(s32[1,10]{1,0:T(1,128)} %pair_ref.1, bf16[11,16,1280]{2,1,0:T(8,128)(2,1)} %shard_map.82.panels_hbm, bf16[1280,512]{1,0:T(8,128)(2,1)} %constant.11.clone.lag_hbm, f32[1,10,8,8,401]{4,3,2,1,0:T(8,128)} %stack_hbm.1), custom_call_target="tpu_custom_call" | custom-call | tf_op jit(solution)/shard_map/pallas_call | solution.py:339

commit v4 on v1

--- a/solution.py
+++ b/solution.py
@@ -20,9 +20,10 @@
 LANE = 128
 BLOCKS = -(-BINS // LANE)
 WIDTH = BLOCKS * LANE
-CHUNK = 512
+CHUNK = 256
 CHUNKS = -(-SAMPLES // CHUNK)
 LAGS_PAD = 512
+TALL_BYTES = 10 << 20
 
 MESH = pl.DeviceIdType.MESH
 
@@ -45,16 +46,19 @@
 def tables():
     dft = interleave(*waves(np.arange(CHUNK, dtype=np.int64))).astype(ml_dtypes.bfloat16)
     turn_real, turn_imag = waves(CHUNK * np.arange(CHUNKS, dtype=np.int64))
-    turns = np.stack([turn_real, turn_imag]).astype(np.float32)
     spots = np.arange(WIDTH)
-    inside = (spots[:, None] < BINS) & (spots[None, :] < BINS)
-    near = (np.abs(spots[:, None] - spots[None, :]) <= HALF) & inside
-    counts = np.maximum(near.sum(axis=0, keepdims=True), 1)
-    band = near.astype(ml_dtypes.bfloat16)
-    inverse = (1.0 / counts).astype(np.float32)
+    low, high = np.maximum(spots - HALF, 0), np.minimum(spots + HALF, BINS - 1)
+    counts = np.maximum(high - low + 1, 1)[None]
+    turns = np.concatenate([turn_real, turn_imag, 1.0 / counts], axis=0)
+    turns = np.pad(turns, ((0, -turns.shape[0] % 8), (0, 0))).astype(np.float32)
     lag_real, lag_imag = waves(np.arange(LAGS, dtype=np.int64) - (LAGS - 1) // 2)
     lag = np.pad(interleave(lag_real, lag_imag).T, ((0, 0), (0, LAGS_PAD - LAGS)))
-    return dft, turns, band, inverse, lag.astype(ml_dtypes.bfloat16)
+    return dft, turns, lag.astype(ml_dtypes.bfloat16)
+
+
+def tall(table):
+    rows = TALL_BYTES // (table.shape[1] * table.dtype.itemsize)
+    return np.pad(table, ((0, rows - table.shape[0]), (0, 0)))
 
 
 def spectrum_of(x_ref, dft_ref, turns_ref):
@@ -78,8 +82,8 @@
         imag_part = jnp.zeros((rows, LANE), jnp.float32)
         for chunk in range(CHUNKS):
             own = part[rows * chunk : rows * (chunk + 1)]
-            turn_real = turns_ref[0, chunk : chunk + 1, bins]
-            turn_imag = turns_ref[1, chunk : chunk + 1, bins]
+            turn_real = turns_ref[chunk : chunk + 1, bins]
+            turn_imag = turns_ref[CHUNKS + chunk : CHUNKS + chunk + 1, bins]
             real_part = real_part + (own[:, :LANE] * turn_real - own[:, LANE:] * turn_imag)
             imag_part = imag_part + (own[:, :LANE] * turn_imag + own[:, LANE:] * turn_real)
         result.append((real_part, imag_part))
@@ -87,17 +91,17 @@
 
 
 def flag_column(mask_ref, rows):
-    chans, segs = mask_ref.shape
+    segs, chans = mask_ref.shape
     place = lax.broadcasted_iota(jnp.int32, (rows, LANE), 0)
     column = jnp.zeros((rows, LANE), jnp.float32)
     for seg in range(segs):
         for chan in range(chans):
-            flag = mask_ref[chan, seg].astype(jnp.float32)
+            flag = mask_ref[seg, chan].astype(jnp.float32)
             column = jnp.where(place == seg * chans + chan, flag, column)
     return column
 
 
-def whitened_blocks(mask_ref, x_ref, dft_ref, turns_ref, band_ref, inverse_ref):
+def whitened_blocks(mask_ref, x_ref, dft_ref, turns_ref, band_ref):
     rows = x_ref.shape[0]
     spectrum = spectrum_of(x_ref, dft_ref, turns_ref)
     power = jnp.concatenate([re * re + im * im for re, im in spectrum], axis=1)
@@ -106,7 +110,7 @@
     sums = jnp.dot(
         jnp.concatenate([high, low], axis=0), band_ref[...], preferred_element_type=jnp.float32
     )
-    smooth = (sums[:rows] + sums[rows:]) * inverse_ref[...]
+    smooth = (sums[:rows] + sums[rows:]) * turns_ref[2 * CHUNKS : 2 * CHUNKS + 1]
     flags = flag_column(mask_ref, rows)
     scale = lax.rsqrt(smooth + EPSILON)
     result = []
@@ -121,9 +125,16 @@
 
 
 def exchange(
-    panel_count, reach, mask_ref, x_ref, dft_ref, turns_ref, band_ref, inverse_ref,
-    out_ref, send_sem, forward_sem, recv_sem,
+    panel_count, reach, mask_ref, x_ref, dft_hbm, turns_hbm,
+    out_ref, dft_ref, turns_ref, band_ref, load_sem, send_sem, forward_sem, recv_sem,
 ):
+    loads = [
+        pltpu.make_async_copy(dft_hbm.at[pl.ds(0, CHUNK)], dft_ref, load_sem.at[0]),
+        pltpu.make_async_copy(turns_hbm.at[pl.ds(0, turns_ref.shape[0])], turns_ref, load_sem.at[1]),
+    ]
+    for load in loads:
+        load.start()
+
     me = lax.axis_index("row")
     chips = panel_count // 2
     chip = me // 2
@@ -138,7 +149,16 @@
         pl.semaphore_signal(barrier, inc=1, device_id=same_core(offset), device_id_type=MESH)
     pl.semaphore_signal(barrier, inc=1, device_id=sibling, device_id_type=MESH)
 
-    blocks = whitened_blocks(mask_ref, x_ref, dft_ref, turns_ref, band_ref, inverse_ref)
+    for block in range(BLOCKS):
+        shape = (WIDTH, LANE)
+        gap = lax.broadcasted_iota(jnp.int32, shape, 0) - lax.broadcasted_iota(jnp.int32, shape, 1)
+        near = jnp.abs(gap - LANE * block) <= HALF
+        band_ref[:, LANE * block : LANE * (block + 1)] = jnp.where(near, 1.0, 0.0).astype(
+            jnp.bfloat16
+        )
+    for load in loads:
+        load.wait()
+    blocks = whitened_blocks(mask_ref, x_ref, dft_ref, turns_ref, band_ref)
     own = core + 1
     for block, (re, im) in enumerate(blocks):
         first = 2 * LANE * block
@@ -249,24 +269,29 @@
     rows = chans * segs
     offsets = pair_table.shape[1]
     reach = (offsets - 2) // 2
-    dft, turns, band, inverse, lag = tables()
+    dft, turns, lag = tables()
     x = jnp.transpose(traces, (1, 0, 2)).reshape(rows, samples)
     vmem = pl.BlockSpec(memory_space=pltpu.VMEM)
+    hbm = pl.BlockSpec(memory_space=pltpu.HBM)
     smem = pl.BlockSpec(memory_space=pltpu.SMEM)
     panels = pl.pallas_call(
         functools.partial(exchange, panel_count, reach),
         out_shape=jax.ShapeDtypeStruct((offsets + 1, rows, 2 * WIDTH), jnp.bfloat16),
-        in_specs=[smem] + [vmem] * 5,
+        in_specs=[smem, vmem, hbm, hbm],
         out_specs=vmem,
         scratch_shapes=[
+            pltpu.VMEM(dft.shape, jnp.bfloat16),
+            pltpu.VMEM(turns.shape, jnp.float32),
+            pltpu.VMEM((WIDTH, WIDTH), jnp.bfloat16),
+            pltpu.SemaphoreType.DMA((2,)),
             pltpu.SemaphoreType.DMA((reach + 2,)),
             pltpu.SemaphoreType.DMA((reach + 2,)),
             pltpu.SemaphoreType.DMA((offsets + 1,)),
         ],
         compiler_params=pltpu.CompilerParams(
-            collective_id=0, has_side_effects=True, vmem_limit_bytes=32 << 20
+            collective_id=0, has_side_effects=True, vmem_limit_bytes=50 << 20
         ),
-    )(valid_mask, x, jnp.asarray(dft), jnp.asarray(turns), jnp.asarray(band), jnp.asarray(inverse))
+    )(valid_mask.T, x, jnp.asarray(tall(dft)), jnp.asarray(tall(turns)))
     group = max(size for size in range(1, 7) if offsets % size == 0)
     tile = (1, group, chans, chans, stack_in.shape[4])
     return pl.pallas_call(

time: 21.2 us -> 18.1 us (0.85); the launches traced: 20.8 us -> 17.9 us
  local copies, waits for them, and re-layouts: 5.84 us -> 1.72 us
  Pallas kernels: 14.9 us -> 16.1 us
    unnamed x15 -> x8, local copies, waits for them, and re-layouts: 4.8 us -> 0.69 us
    pallas_call x1, Pallas kernels: 12 us -> 13.3 us  [shards(): pl.pallas_call(functools.partial(exchange, panel_count, reach), out_shape...]
where the time goes in v4:
time: 18.1 us; the launch traced here: 17.9 us
  Pallas kernels  16.1 us (89%)
  local copies, waits for them, and re-layouts  1.72 us (10%)
    pallas_call x1, Pallas kernels, shards(): pl.pallas_call(functools.partial(exchange, panel_count, reach), out_shape...  13.3 us
    pallas_call x1, Pallas kernels, shards(): pl.pallas_call(functools.partial(correlate, panel_count), out_shape=jax.S...  2.84 us
    transpose x1, local copies, waits for them, and re-layouts, shards(): x = jnp.transpose(traces, (1, 0, 2)).reshape(rows, samples)  1.03 us
    unnamed x8, local copies, waits for them, and re-layouts  0.69 us

profile of v4, /device:TPU:0, one launch (start us, length us, event | category | flops | bytes accessed | tf_op | source)
XLA Modules:
  0.0 17.9 jit_solution(13582532063883879992)
XLA Ops:
  0.0 1.0 %copy.10 = bf16[2,8,12000]{2,1,0:T(8,128)(2,1)S(1)} copy(bf16[2,8,12000]{2,0,1:T(2,128)(2,1)} %bitcast.7) | data formatting | bytes 768000 | tf_op jit(solution)/shard_map/transpose | solution.py:273
  1.0 0.0 copy-start.2
  1.0 0.7 %copy-done.2 = s32[8,2]{0,1:T(2,128)S(1)} copy-done((s32[8,2]{0,1:T(2,128)S(1)}, s32[8,2]{0,1:T(2,128)}, u32[]{:S(2)}) %copy-start.2) | copy-done | bytes 88
  1.7 0.0 copy-start
  1.7 0.0 copy-start.1
  1.7 0.0 copy-start.3
  1.7 13.3 %shard_map.73.panels_ref = bf16[11,16,1280]{2,1,0:T(8,128)(2,1)S(1)} custom-call(s32[2,8]{1,0:T(2,128)S(1)} %bitcast.6, bf16[16,12000]{1,0:T(8,128)(2,1)S(1)} %bitcast.5, bf16[4096,1280]{1,0:T(8,128)(2,1)} %constant.6.clone.dft_hbm, f32[4096,640]{1,0:T(8,128)} %constant.7.clone.turns_hbm), custom_call_target="tpu_custom_call" | custom-call | tf_op jit(solution)/shard_map/pallas_call | solution.py:277
  15.0 0.0 copy-done
  15.0 0.0 copy-done.1
  15.0 0.0 copy-done.3
  15.0 2.8 %shard_map.74 = f32[1,10,8,8,401]{4,3,2,1,0:T(8,128)} custom-call(s32[1,10]{1,0:T(1,128)S(1)} %copy-done.3, bf16[11,16,1280]{2,1,0:T(8,128)(2,1)S(1)} %shard_map.73.panels_ref, bf16[1280,512]{1,0:T(8,128)(2,1)S(1)} %copy-done.1, f32[1,10,8,8,401]{4,3,2,1,0:T(8,128)S(1)} %copy-done), custom_call_target="tpu_custom_call" | custom-call | tf_op jit(solution)/shard_map/pallas_call | solution.py:297
Async XLA Ops:
  1.0 0.7 %copy-start.2 = (s32[8,2]{0,1:T(2,128)S(1)}, s32[8,2]{0,1:T(2,128)}, u32[]{:S(2)}) copy-start(s32[8,2]{0,1:T(2,128)} %param.8) | copy-start | bytes 196
  1.7 13.3 %copy-start = (f32[1,10,8,8,401]{4,3,2,1,0:T(8,128)S(1)}, f32[1,10,8,8,401]{4,3,2,1,0:T(8,128)}, u32[]{:S(2)}) copy-start(f32[1,10,8,8,401]{4,3,2,1,0:T(8,128)} %stack_ref.1) | copy-start | bytes 3079684
  1.7 13.3 %copy-start.1 = (bf16[1280,512]{1,0:T(8,128)(2,1)S(1)}, bf16[1280,512]{1,0:T(8,128)(2,1)}, u32[]{:S(2)}) copy-start(bf16[1280,512]{1,0:T(8,128)(2,1)} %constant.8.clone.lag_ref) | copy-start | bytes 3932164
  1.7 13.3 %copy-start.3 = (s32[1,10]{1,0:T(1,128)S(1)}, s32[1,10]{1,0:T(1,128)}, u32[]{:S(2)}) copy-start(s32[1,10]{1,0:T(1,128)} %pair_ref.1) | copy-start | bytes 124

commit v5 on v4

--- a/solution.py
+++ b/solution.py
@@ -126,7 +126,8 @@
 
 def exchange(
     panel_count, reach, mask_ref, x_ref, dft_hbm, turns_hbm,
-    out_ref, dft_ref, turns_ref, band_ref, load_sem, send_sem, forward_sem, recv_sem,
+    out_ref, dft_ref, turns_ref, band_ref, load_sem, send_sem,
+    column_sem, relay_sem, forward_sem, recv_sem,
 ):
     loads = [
         pltpu.make_async_copy(dft_hbm.at[pl.ds(0, CHUNK)], dft_ref, load_sem.at[0]),
@@ -177,52 +178,77 @@
             device_id_type=MESH,
         )
 
-    direct = [
-        copy(own, 2 * step + core + 1, send_sem.at[step + 1], same_core(-step))
-        for step in range(reach, 0, -1)
+    side = lax.rem(chip, 2)
+    partner = {"row": 2 * (chip + 1 - 2 * side) + core}
+    nodes = reach // 2
+    columns = [
+        copy(own, 4 * step + core + 1, column_sem.at[step - 1], same_core(-2 * step))
+        for step in range(1, nodes + 1)
     ]
+
+    def relay(step):
+        target = 4 * step - 1 + core
+        return copy(4 * (step - side) + core + 1, target, relay_sem.at[step - 1], partner)
+
+    def forward(slot, step):
+        return copy(slot, slot, forward_sem.at[step], sibling)
+
     back = copy(own, 0, send_sem.at[0], same_core(1))
     beside = copy(own, own, send_sem.at[1], sibling)
-    for sent in direct:
+    for sent in columns:
         sent.start()
 
+    @pl.when(side == 1)
+    def _():
+        relay(1).start()
+
     @pl.when(core == 1)
     def _():
         back.start()
 
     beside.start()
 
-    forwards = []
-    back_forward = copy(0, 0, forward_sem.at[0], sibling)
-    for step in range(1, reach + 1):
-        slot = 2 * step + core + 1
-        passed = copy(slot, slot, forward_sem.at[step], sibling)
+    for step in range(1, nodes + 1):
+        passed = forward(4 * step + core + 1, 2 * step)
+        passed.wait_recv()
+        if step < nodes:
+            relay(step + side).start()
+        else:
+
+            @pl.when(side == 0)
+            def _():
+                relay(nodes).start()
+
+        passed.start()
+    for step in range(1, nodes + 1):
+        passed = forward(4 * step - 1 + core, 2 * step - 1)
         passed.wait_recv()
         passed.start()
-        forwards.append(passed)
-        if step == 1:
-
-            @pl.when(core == 1)
-            def _():
-                back_forward.wait_recv()
-                back_forward.start()
+
+    @pl.when(core == 1)
+    def _():
+        forward(0, 0).wait_recv()
+        forward(0, 0).start()
 
     copy(2 - core, 2 - core, send_sem.at[1], sibling).wait_recv()
     for step in range(1, reach + 1):
-        slot = 2 * step + 2 - core
-        copy(slot, slot, forward_sem.at[step], sibling).wait_recv()
+        forward(2 * step + 2 - core, step).wait_recv()
 
     @pl.when(core == 0)
     def _():
-        back_forward.wait_recv()
-
-    for sent in direct + [beside] + forwards:
+        forward(0, 0).wait_recv()
+
+    for sent in columns + [beside]:
         sent.wait_send()
+    for step in range(1, nodes + 1):
+        relay(step).wait_send()
+    for step in range(1, reach + 1):
+        forward(own, step).wait_send()
 
     @pl.when(core == 1)
     def _():
         back.wait_send()
-        back_forward.wait_send()
+        forward(0, 0).wait_send()
 
 
 def correlate(panel_count, pair_ref, panels_ref, lag_ref, stack_ref, out_ref, cross_ref):
@@ -284,8 +310,10 @@
             pltpu.VMEM(turns.shape, jnp.float32),
             pltpu.VMEM((WIDTH, WIDTH), jnp.bfloat16),
             pltpu.SemaphoreType.DMA((2,)),
-            pltpu.SemaphoreType.DMA((reach + 2,)),
-            pltpu.SemaphoreType.DMA((reach + 2,)),
+            pltpu.SemaphoreType.DMA((2,)),
+            pltpu.SemaphoreType.DMA((reach // 2,)),
+            pltpu.SemaphoreType.DMA((reach // 2,)),
+            pltpu.SemaphoreType.DMA((reach + 1,)),
             pltpu.SemaphoreType.DMA((offsets + 1,)),
         ],
         compiler_params=pltpu.CompilerParams(

time: 18.1 us -> 17.7 us (0.978)
  Pallas kernels: 16.1 us -> 15.7 us
    pallas_call x1, Pallas kernels: 13.3 us -> 12.9 us  [shards(): pl.pallas_call(functools.partial(exchange, panel_count, reach), out_shape...]
where the time goes in v5:
time: 17.7 us; the launch traced here: 17.5 us
  Pallas kernels  15.7 us (89%)
  local copies, waits for them, and re-layouts  1.72 us (10%)
    pallas_call x1, Pallas kernels, shards(): pl.pallas_call(functools.partial(exchange, panel_count, reach), out_shape...  12.9 us
    pallas_call x1, Pallas kernels, shards(): pl.pallas_call(functools.partial(correlate, panel_count), out_shape=jax.S...  2.85 us
    transpose x1, local copies, waits for them, and re-layouts, shards(): x = jnp.transpose(traces, (1, 0, 2)).reshape(rows, samples)  1.03 us
    unnamed x8, local copies, waits for them, and re-layouts  0.69 us

profile of v5, /device:TPU:0, one launch (start us, length us, event | category | flops | bytes accessed | tf_op | source)
XLA Modules:
  0.0 17.5 jit_solution(14228442024680698210)
XLA Ops:
  0.0 1.0 %copy.10 = bf16[2,8,12000]{2,1,0:T(8,128)(2,1)S(1)} copy(bf16[2,8,12000]{2,0,1:T(2,128)(2,1)} %bitcast.7) | data formatting | bytes 768000 | tf_op jit(solution)/shard_map/transpose | solution.py:299
  1.0 0.0 copy-start.2
  1.0 0.7 %copy-done.2 = s32[8,2]{0,1:T(2,128)S(1)} copy-done((s32[8,2]{0,1:T(2,128)S(1)}, s32[8,2]{0,1:T(2,128)}, u32[]{:S(2)}) %copy-start.2) | copy-done | bytes 88
  1.7 0.0 copy-start
  1.7 0.0 copy-start.1
  1.7 0.0 copy-start.3
  1.7 12.9 %shard_map.73.panels_ref = bf16[11,16,1280]{2,1,0:T(8,128)(2,1)S(1)} custom-call(s32[2,8]{1,0:T(2,128)S(1)} %bitcast.6, bf16[16,12000]{1,0:T(8,128)(2,1)S(1)} %bitcast.5, bf16[4096,1280]{1,0:T(8,128)(2,1)} %constant.6.clone.dft_hbm, f32[4096,640]{1,0:T(8,128)} %constant.7.clone.turns_hbm), custom_call_target="tpu_custom_call" | custom-call | tf_op jit(solution)/shard_map/pallas_call | solution.py:303
  14.6 0.0 copy-done
  14.6 0.0 copy-done.1
  14.6 0.0 copy-done.3
  14.6 2.9 %shard_map.74 = f32[1,10,8,8,401]{4,3,2,1,0:T(8,128)} custom-call(s32[1,10]{1,0:T(1,128)S(1)} %copy-done.3, bf16[11,16,1280]{2,1,0:T(8,128)(2,1)S(1)} %shard_map.73.panels_ref, bf16[1280,512]{1,0:T(8,128)(2,1)S(1)} %copy-done.1, f32[1,10,8,8,401]{4,3,2,1,0:T(8,128)S(1)} %copy-done), custom_call_target="tpu_custom_call" | custom-call | tf_op jit(solution)/shard_map/pallas_call | solution.py:325
Async XLA Ops:
  1.0 0.7 %copy-start.2 = (s32[8,2]{0,1:T(2,128)S(1)}, s32[8,2]{0,1:T(2,128)}, u32[]{:S(2)}) copy-start(s32[8,2]{0,1:T(2,128)} %param.8) | copy-start | bytes 196
  1.7 12.9 %copy-start = (f32[1,10,8,8,401]{4,3,2,1,0:T(8,128)S(1)}, f32[1,10,8,8,401]{4,3,2,1,0:T(8,128)}, u32[]{:S(2)}) copy-start(f32[1,10,8,8,401]{4,3,2,1,0:T(8,128)} %stack_ref.1) | copy-start | bytes 3079684
  1.7 12.9 %copy-start.1 = (bf16[1280,512]{1,0:T(8,128)(2,1)S(1)}, bf16[1280,512]{1,0:T(8,128)(2,1)}, u32[]{:S(2)}) copy-start(bf16[1280,512]{1,0:T(8,128)(2,1)} %constant.8.clone.lag_ref) | copy-start | bytes 3932164
  1.7 12.9 %copy-start.3 = (s32[1,10]{1,0:T(1,128)S(1)}, s32[1,10]{1,0:T(1,128)}, u32[]{:S(2)}) copy-start(s32[1,10]{1,0:T(1,128)} %pair_ref.1) | copy-start | bytes 124

commit v6 on v5

--- a/solution.py
+++ b/solution.py
@@ -24,6 +24,7 @@
 CHUNKS = -(-SAMPLES // CHUNK)
 LAGS_PAD = 512
 TALL_BYTES = 10 << 20
+LOADS = 4
 
 MESH = pl.DeviceIdType.MESH
 
@@ -130,9 +131,14 @@
     column_sem, relay_sem, forward_sem, recv_sem,
 ):
     loads = [
-        pltpu.make_async_copy(dft_hbm.at[pl.ds(0, CHUNK)], dft_ref, load_sem.at[0]),
-        pltpu.make_async_copy(turns_hbm.at[pl.ds(0, turns_ref.shape[0])], turns_ref, load_sem.at[1]),
+        pltpu.make_async_copy(turns_hbm.at[pl.ds(0, turns_ref.shape[0])], turns_ref, load_sem.at[0])
     ]
+    depth = CHUNK // LOADS
+    for piece in range(LOADS):
+        lines = pl.ds(depth * piece, depth)
+        loads.append(
+            pltpu.make_async_copy(dft_hbm.at[lines], dft_ref.at[lines], load_sem.at[1 + piece])
+        )
     for load in loads:
         load.start()
 
@@ -309,7 +315,7 @@
             pltpu.VMEM(dft.shape, jnp.bfloat16),
             pltpu.VMEM(turns.shape, jnp.float32),
             pltpu.VMEM((WIDTH, WIDTH), jnp.bfloat16),
-            pltpu.SemaphoreType.DMA((2,)),
+            pltpu.SemaphoreType.DMA((1 + LOADS,)),
             pltpu.SemaphoreType.DMA((2,)),
             pltpu.SemaphoreType.DMA((reach // 2,)),
             pltpu.SemaphoreType.DMA((reach // 2,)),

time: 17.7 us -> 17.7 us (level)
  no operation moved by 1% of the time
where the time goes in v6:
time: 17.7 us; the launch traced here: 17.5 us
  Pallas kernels  15.8 us (89%)
  local copies, waits for them, and re-layouts  1.72 us (10%)
    pallas_call x1, Pallas kernels, shards(): pl.pallas_call(functools.partial(exchange, panel_count, reach), out_shape...  12.9 us
    pallas_call x1, Pallas kernels, shards(): pl.pallas_call(functools.partial(correlate, panel_count), out_shape=jax.S...  2.84 us
    transpose x1, local copies, waits for them, and re-layouts, shards(): x = jnp.transpose(traces, (1, 0, 2)).reshape(rows, samples)  1.03 us
    unnamed x8, local copies, waits for them, and re-layouts  0.69 us

profile of v6, /device:TPU:0, one launch (start us, length us, event | category | flops | bytes accessed | tf_op | source)
XLA Modules:
  0.0 17.5 jit_solution(18372287199922748400)
XLA Ops:
  0.0 1.0 %copy.10 = bf16[2,8,12000]{2,1,0:T(8,128)(2,1)S(1)} copy(bf16[2,8,12000]{2,0,1:T(2,128)(2,1)} %bitcast.7) | data formatting | bytes 768000 | tf_op jit(solution)/shard_map/transpose | solution.py:305
  1.0 0.0 copy-start.2
  1.0 0.7 %copy-done.2 = s32[8,2]{0,1:T(2,128)S(1)} copy-done((s32[8,2]{0,1:T(2,128)S(1)}, s32[8,2]{0,1:T(2,128)}, u32[]{:S(2)}) %copy-start.2) | copy-done | bytes 88
  1.7 0.0 copy-start
  1.7 0.0 copy-start.1
  1.7 0.0 copy-start.3
  1.7 12.9 %shard_map.73.panels_ref = bf16[11,16,1280]{2,1,0:T(8,128)(2,1)S(1)} custom-call(s32[2,8]{1,0:T(2,128)S(1)} %bitcast.6, bf16[16,12000]{1,0:T(8,128)(2,1)S(1)} %bitcast.5, bf16[4096,1280]{1,0:T(8,128)(2,1)} %constant.6.clone.dft_hbm, f32[4096,640]{1,0:T(8,128)} %constant.7.clone.turns_hbm), custom_call_target="tpu_custom_call" | custom-call | tf_op jit(solution)/shard_map/pallas_call | solution.py:309
  14.7 0.0 copy-done
  14.7 0.0 copy-done.1
  14.7 0.0 copy-done.3
  14.7 2.8 %shard_map.74 = f32[1,10,8,8,401]{4,3,2,1,0:T(8,128)} custom-call(s32[1,10]{1,0:T(1,128)S(1)} %copy-done.3, bf16[11,16,1280]{2,1,0:T(8,128)(2,1)S(1)} %shard_map.73.panels_ref, bf16[1280,512]{1,0:T(8,128)(2,1)S(1)} %copy-done.1, f32[1,10,8,8,401]{4,3,2,1,0:T(8,128)S(1)} %copy-done), custom_call_target="tpu_custom_call" | custom-call | tf_op jit(solution)/shard_map/pallas_call | solution.py:331
Async XLA Ops:
  1.0 0.7 %copy-start.2 = (s32[8,2]{0,1:T(2,128)S(1)}, s32[8,2]{0,1:T(2,128)}, u32[]{:S(2)}) copy-start(s32[8,2]{0,1:T(2,128)} %param.8) | copy-start | bytes 196
  1.7 13.0 %copy-start = (f32[1,10,8,8,401]{4,3,2,1,0:T(8,128)S(1)}, f32[1,10,8,8,401]{4,3,2,1,0:T(8,128)}, u32[]{:S(2)}) copy-start(f32[1,10,8,8,401]{4,3,2,1,0:T(8,128)} %stack_ref.1) | copy-start | bytes 3079684
  1.7 13.0 %copy-start.1 = (bf16[1280,512]{1,0:T(8,128)(2,1)S(1)}, bf16[1280,512]{1,0:T(8,128)(2,1)}, u32[]{:S(2)}) copy-start(bf16[1280,512]{1,0:T(8,128)(2,1)} %constant.8.clone.lag_ref) | copy-start | bytes 3932164
  1.7 13.0 %copy-start.3 = (s32[1,10]{1,0:T(1,128)S(1)}, s32[1,10]{1,0:T(1,128)}, u32[]{:S(2)}) copy-start(s32[1,10]{1,0:T(1,128)} %pair_ref.1) | copy-start | bytes 124
